TPU v7x, 1024 devices: a whole 4x8x16 slice. The times are simulated.
1024 devices in a mesh: row: 64 (over y_lo, z), col: 16 (over y_hi, x, core).
Axes of the slice: x: 4, y: 8 (y_hi: 2, y_lo: 4; y = y_hi * 4 + y_lo), z: 16, core: 2. Of those that a mesh axis runs over, the one named last changes fastest.
Arguments:
- current_block: float32 [8, 131072], P(None, ('row', 'col'))
- prior_blocks: float32 [32, 131072], P(None, ('row', 'col'))
- diagonal: float32 [131072], P(('row', 'col')), may hold values from 1 to 4
- stored_tiles: float32 [64, 16, 8, 128, 128], P('row', 'col'), may hold values from -0.1875 to 0.1875
- tile_coords: int32 [64, 16, 2, 8], P('row', 'col'), may hold values from 0 to 63, as said below
- tile_counts: int32 [64, 16], P('row', 'col'), may hold values from 2 to 8, as said below
Outputs:
- new_blocks: float32 [16, 131072], P(None, ('row', 'col'))
Inputs may be any that keep to these rules, and one draw needn't show every extreme that they name: `tile_counts`: live slots of one device; some device holds 8. `tile_coords`: index 0 lies below 16, index 1 below 64; positions may repeat.
All inputs are finite; a program needn't handle non-finite values.
Results may differ from a plain program's by a relative error of at most 0.0003.
Values sent between devices are 32-bit elements; how exact they have to be, the bound alone decides.
A program may use at most 32 MiB of HBM per device.

v0:
```python
import jax
import jax.numpy as jnp
from jax import lax
from jax.sharding import PartitionSpec as P

STEPS = 2


HIGH = lax.Precision.HIGHEST


def tile_terms(tile_block, rows_hot, cols_hot, row_vector, column_vector):
    tile_width = tile_block.shape[-1]
    vec_rows = row_vector.shape[0]
    row_grid = row_vector.reshape(vec_rows, rows_hot.shape[1], tile_width)
    col_grid = column_vector.reshape(vec_rows, cols_hot.shape[1], tile_width)
    row_inputs = jnp.einsum("ta,kai->tki", rows_hot, row_grid, precision=HIGH)
    col_inputs = jnp.einsum("tb,kbi->tki", cols_hot, col_grid, precision=HIGH)
    to_rows = jnp.einsum("tki,tji->tkj", col_inputs, tile_block, precision=HIGH)
    to_cols = jnp.einsum("tki,tij->tkj", row_inputs, tile_block, precision=HIGH)
    row_terms = jnp.einsum("ta,tkj->kaj", rows_hot, to_rows, precision=HIGH).reshape(vec_rows, -1)
    return (row_terms, to_cols)


def column_total(to_cols, cols_hot):
    vec_rows = to_cols.shape[1]
    col_terms = jnp.einsum("tb,tkj->kbj", cols_hot, to_cols, precision=HIGH).reshape(vec_rows, -1)
    return lax.psum_scatter(col_terms, "row", scatter_dimension=1, tiled=True)


def grid_total(values):
    return lax.psum(values, ("row", "col"))


def orthonormal(window, current, image_block, vector_len, combine_sums):
    basis_rows = jnp.concatenate([window, current], axis=0)
    projection = combine_sums(jnp.dot(basis_rows, image_block.T, precision=HIGH)) / vector_len
    remainder = image_block - jnp.dot(projection.T, basis_rows, precision=HIGH)
    gram_matrix = combine_sums(jnp.dot(remainder, remainder.T, precision=HIGH)) / vector_len
    lower_factor = jnp.linalg.cholesky(gram_matrix)
    return lax.linalg.triangular_solve(lower_factor, remainder, left_side=True, lower=True)


def body(current_block, prior_blocks, diagonal, stored_tiles, tile_coords, tile_counts):
    tile_block = stored_tiles[0, 0]
    tile_where = tile_coords[0, 0]
    slot_count = tile_counts[0, 0]
    tile_width = tile_block.shape[-1]
    slot_total = tile_block.shape[0]
    block_width = current_block.shape[0]
    piece_len = current_block.shape[1]
    row_devices = lax.axis_size("row")
    col_devices = lax.axis_size("col")
    vector_len = float(piece_len * row_devices * col_devices)
    live_slots = (jnp.arange(slot_total, dtype=jnp.int32) < slot_count).astype(jnp.float32)
    row_tiles = col_devices * piece_len // tile_width
    col_tiles = row_devices * piece_len // tile_width
    rows_hot = (tile_where[0][:, None] == jnp.arange(row_tiles, dtype=jnp.int32)[None, :]).astype(
        jnp.float32
    ) * live_slots[:, None]
    cols_hot = (tile_where[1][:, None] == jnp.arange(col_tiles, dtype=jnp.int32)[None, :]).astype(
        jnp.float32
    ) * live_slots[:, None]
    produced = []
    window = prior_blocks
    current = current_block
    for step_index in range(STEPS):
        row_vector = lax.all_gather(current, "col", axis=1, tiled=True)
        column_vector = lax.all_gather(current, "row", axis=1, tiled=True)
        row_terms, to_cols = tile_terms(tile_block, rows_hot, cols_hot, row_vector, column_vector)
        row_share = lax.psum_scatter(row_terms, "col", scatter_dimension=1, tiled=True)
        col_share = column_total(to_cols, cols_hot)
        image_block = row_share + col_share + diagonal[None, :] * current
        fresh = orthonormal(window, current, image_block, vector_len, grid_total)
        produced.append(fresh)
        window = jnp.concatenate([window[block_width:], current], axis=0)
        current = fresh
    return jnp.concatenate(produced, axis=0)


def solution(mesh):
    in_specs = (
        P(None, ("row", "col")),
        P(None, ("row", "col")),
        P(("row", "col")),
        P("row", "col", None, None, None),
        P("row", "col", None, None),
        P("row", "col"),
    )
    out_specs = P(None, ("row", "col"))
    return jax.shard_map(body, mesh=mesh, in_specs=in_specs, out_specs=out_specs, check_vma=False)
```

profile of v0, /device:TPU:1, one launch (start us, length us, event | category | flops | bytes accessed | tf_op | source)
XLA Modules:
  0.0 1641.4 jit_solution(1771618771761566464)
XLA Ops:
  7.3 0.7 copy-done.6
  8.0 138.5 %all_gather.12 = f32[8,8192]{1,0:T(8,128)S(1)} all-gather(f32[8,128]{1,0:T(8,128)S(1)} %copy-done.1), channel_id=1, replica_groups=mesh['row'=64,'col'=16] {'row'}, dimensions={1}, use_global_device_ids=true | all-gather | bytes 266240 | tf_op jit(solution)/shard_map/all_gather | solution.py:69
  146.7 0.9 fusion.6
  148.7 57.6 %all_gather.13 = f32[8,2048]{1,0:T(8,128)S(1)} all-gather(f32[8,128]{1,0:T(8,128)S(1)} %copy-done.1), channel_id=1, replica_groups=mesh['row'=64,'col'=16] {'col'}, dimensions={1}, use_global_device_ids=true | all-gather | bytes 69632 | tf_op jit(solution)/shard_map/all_gather | solution.py:68
  207.6 0.8 copy.60
  209.1 50.5 %reduce-scatter.5.cloned.1.call-done = f32[8,128]{1,0:T(8,128)} async-done(((f32[8,2048]{1,0:T(8,128)}), f32[8,128]{1,0:T(8,128)}) %reduce-scatter.5.cloned.1.call-update) | async-done | bytes 4112 | tf_op jit(solution)/shard_map/reduce_scatter | solution.py:71
  259.6 265.6 %reduce-scatter.7.cloned.1.call-done = f32[8,128]{1,0:T(8,128)} async-done(((f32[8,8192]{1,0:T(8,128)}), f32[8,128]{1,0:T(8,128)}) %reduce-scatter.7.cloned.1.call-update) | async-done | bytes 4112 | tf_op jit(solution)/shard_map/reduce_scatter | solution.py:28
  525.2 0.7 constant_dynamic-update-slice_fusion
  526.1 170.4 %psum.28 = f32[40,8]{1,0:T(8,128)S(1)} all-reduce(f32[40,8]{1,0:T(8,128)S(1)} %fusion.91), channel_id=1, replica_groups=mesh['row'=64,'col'=16] {'row','col'}, use_global_device_ids=true, to_apply=%region_2.0 | all-reduce | flops 320 | bytes 2560 | tf_op jit(solution)/shard_map/psum | solution.py:32
  696.8 117.3 %psum.29 = f32[8,8]{0,1:T(8,128)S(1)} all-reduce(f32[8,8]{0,1:T(8,128)S(1)} %fusion.92), channel_id=1, replica_groups=mesh['row'=64,'col'=16] {'row','col'}, use_global_device_ids=true, to_apply=%region_3.0 | all-reduce | flops 64 | bytes 512 | tf_op jit(solution)/shard_map/psum | solution.py:32
  814.2 0.7 cholesky.44
  815.6 0.6 fusion.29
  817.1 28.8 %all_gather.15 = f32[8,2048]{1,0:T(8,128)S(1)} all-gather(f32[8,128]{1,0:T(8,128)S(1)} %fusion.33), channel_id=1, replica_groups=mesh['row'=64,'col'=16] {'col'}, dimensions={1}, use_global_device_ids=true | all-gather | bytes 69632 | tf_op jit(solution)/shard_map/all_gather | solution.py:68
  845.9 119.4 %all_gather.14 = f32[8,8192]{1,0:T(8,128)S(1)} all-gather(f32[8,128]{1,0:T(8,128)S(1)} %fusion.33), channel_id=1, replica_groups=mesh['row'=64,'col'=16] {'row'}, dimensions={1}, use_global_device_ids=true | all-gather | bytes 266240 | tf_op jit(solution)/shard_map/all_gather | solution.py:69
  966.4 0.9 fusion.2
  968.9 0.8 copy.59
  969.7 106.7 %reduce-scatter.9.cloned.1.call-done = f32[8,128]{1,0:T(8,128)} async-done(((f32[8,2048]{1,0:T(8,128)}), f32[8,128]{1,0:T(8,128)}) %reduce-scatter.9.cloned.1.call-update) | async-done | bytes 4112 | tf_op jit(solution)/shard_map/reduce_scatter | solution.py:71
  1076.5 265.8 %reduce-scatter.11.cloned.1.call-done = f32[8,128]{1,0:T(8,128)} async-done(((f32[8,8192]{1,0:T(8,128)}), f32[8,128]{1,0:T(8,128)}) %reduce-scatter.11.cloned.1.call-update) | async-done | bytes 4112 | tf_op jit(solution)/shard_map/reduce_scatter | solution.py:28
  1342.3 0.9 fusion.26
  1343.2 170.4 %psum.30 = f32[40,8]{1,0:T(8,128)S(1)} all-reduce(f32[40,8]{1,0:T(8,128)S(1)} %fusion.26), channel_id=1, replica_groups=mesh['row'=64,'col'=16] {'row','col'}, use_global_device_ids=true, to_apply=%region_8.11 | all-reduce | flops 320 | bytes 2560 | tf_op jit(solution)/shard_map/psum | solution.py:32
  1513.9 117.3 %psum.31 = f32[8,8]{0,1:T(8,128)S(1)} all-reduce(f32[8,8]{0,1:T(8,128)S(1)} %fusion.93), channel_id=1, replica_groups=mesh['row'=64,'col'=16] {'row','col'}, use_global_device_ids=true, to_apply=%region_9.12 | all-reduce | flops 64 | bytes 512 | tf_op jit(solution)/shard_map/psum | solution.py:32
  1631.3 0.7 cholesky.55
  1632.1 0.6 compare_reduce_fusion
  1632.7 0.6 fusion.30
  (56 shorter events, 9.9 us)
Async XLA Ops:
  6.5 140.2 %copy-start = (f32[1,1,8,128,128]{4,3,2,1,0:T(8,128)S(1)}, f32[1,1,8,128,128]{4,3,2,1,0:T(8,128)}, u32[]{:S(2)}) copy-start(f32[1,1,8,128,128]{4,3,2,1,0:T(8,128)} %param.12) | copy-start | bytes 1572868
  6.5 1.4 copy-start.1
  6.5 253.1 %reduce-scatter.5.cloned.1.call-start = ((), (), s32[]{:S(2)}) async-start(), calls=%async_computation.4 | async-start | bytes 69632 | tf_op jit(solution)/shard_map/reduce_scatter | solution.py:71
  7.3 0.7 copy-start.6
  148.7 376.5 %reduce-scatter.7.cloned.1.call-start = ((), (), s32[]{:S(2)}) async-start(), calls=%async_computation.5 | async-start | bytes 266240 | tf_op jit(solution)/shard_map/reduce_scatter | solution.py:28
  208.4 0.7 copy-start.2
  208.4 316.7 %copy-start.5 = (f32[128]{0:T(128)S(1)}, f32[128]{0:T(128)}, u32[]{:S(2)}) copy-start(f32[128]{0:T(128)} %param.11) | copy-start | bytes 1540
  208.5 868.0 %reduce-scatter.9.cloned.1.call-start = ((), (), s32[]{:S(2)}) async-start(), calls=%async_computation.6 | async-start | bytes 69632 | tf_op jit(solution)/shard_map/reduce_scatter | solution.py:71
  968.3 374.0 %reduce-scatter.11.cloned.1.call-start = ((), (), s32[]{:S(2)}) async-start(), calls=%async_computation.7 | async-start | bytes 266240 | tf_op jit(solution)/shard_map/reduce_scatter | solution.py:28
  1343.2 170.4 %copy-start.3 = (f32[8,128]{1,0:T(8,128)S(1)}, f32[8,128]{1,0:T(8,128)}, u32[]{:S(2)}) copy-start(f32[8,128]{1,0:T(8,128)} %reduce-scatter.9.cloned.1.call-done) | copy-start | bytes 12292
  1343.2 170.4 %copy-start.4 = (f32[8,128]{1,0:T(8,128)S(1)}, f32[8,128]{1,0:T(8,128)}, u32[]{:S(2)}) copy-start(f32[8,128]{1,0:T(8,128)} %reduce-scatter.11.cloned.1.call-done) | copy-start | bytes 12292
Sparse Core Ops, SparseCore 0:
  148.8 110.7 reduce-scatter.4
  263.0 262.1 reduce-scatter.6
  968.4 107.9 reduce-scatter.8
  1080.1 262.1 reduce-scatter.10
where the time goes:
time: 1640 us
  blocking collectives  920 us (56%)
  waiting for transfers between devices  689 us (42%)
    psum x4, blocking collectives, grid_total(): return lax.psum(values, ('row', 'col'))  575 us
    reduce_scatter x2, waiting for transfers between devices, column_total(): return lax.psum_scatter(col_terms, 'row', scatter_dimension=1, tiled=True)  531 us
    all_gather x2, blocking collectives, body(): column_vector = lax.all_gather(current, 'row', axis=1, tiled=True)  258 us
    reduce_scatter x2, waiting for transfers between devices, body(): lax.psum_scatter(row_terms, 'col', scatter_dimension=1, tiled=True)  157 us
    all_gather x2, blocking collectives, body(): row_vector = lax.all_gather(current, 'col', axis=1, tiled=True)  86.4 us
  transfers between devices with their start and end apart: 4, of which 4 were waited for; matrix products, arithmetic and copies ran while one was open for 0% of the time, Pallas kernels for 0%

commit v1 on v0

v1 whole, which is shorter than its diff:
```python
import functools

import jax
import jax.numpy as jnp
from jax import lax
from jax.experimental import pallas as pl
from jax.experimental.pallas import tpu as pltpu
from jax.sharding import PartitionSpec as P

MESH = pl.DeviceIdType.MESH
HIGH = lax.Precision.HIGHEST
F32 = jnp.float32
BF16 = jnp.bfloat16

LAYOUT = dict(y_lo=4, z_far=4, y_hi=2, x=4, core=2)
NEAR = 4


class Place:
    def __init__(self, lay):
        self.lay = lay
        self.nz = lay["z_far"] * NEAR
        self.ncol = lay["y_hi"] * lay["x"] * lay["core"]
        self.fold = lay["x"] * lay["core"]
        self.ny = lay["y_lo"] * lay["y_hi"]
        self.r = lax.axis_index("row")
        self.c = lax.axis_index("col")
        self.y = lax.div(self.r, self.nz)
        self.z = lax.rem(self.r, self.nz)
        self.z_far = lax.div(self.z, NEAR)
        self.z_near = lax.rem(self.z, NEAR)
        self.y_hi = lax.div(self.c, self.fold)

    def row_at(self, dy, dz):
        y = lax.rem(self.y + dy, self.lay["y_lo"])
        z = lax.rem(self.z + dz, self.nz)
        return y * self.nz + z

    def at_z(self, dz):
        return (self.row_at(0, dz), self.c)

    def at_far(self, d, dy):
        return (self.row_at(dy, NEAR * d), self.c)

    def at_col(self, k):
        return (self.r, lax.rem(self.c + k, self.ncol))

    def at_fold(self, k):
        inner = lax.rem(self.c, self.fold)
        return (self.r, self.y_hi * self.fold + lax.rem(inner + k, self.fold))

    def at_y(self, k):
        y_lo = self.lay["y_lo"]
        y = lax.rem(self.y_hi * y_lo + self.y + k, self.ny)
        inner = lax.rem(self.c, self.fold)
        return (
            lax.rem(y, y_lo) * self.nz + self.z,
            lax.div(y, y_lo) * self.fold + inner,
        )

    def near_out(self):
        odd = lax.rem(self.z, 2)
        return (1, self.nz - 1, 2 + odd * (self.nz - 4))

    def near_in(self):
        odd = lax.rem(self.z, 2)
        return (self.nz - 1, 1, self.nz - 2 + odd * 4)


def split(values):
    high = values.astype(BF16)
    low = (values - high.astype(F32)).astype(BF16)
    return high, low


def apply_tile(vectors, weights):
    high, low = split(vectors)
    both = jnp.dot(jnp.concatenate([high, low], axis=0), weights, preferred_element_type=F32)
    width = weights.shape[1] // 2
    rows = vectors.shape[0]
    high_part = both[:rows, :width] + both[:rows, width:]
    return high_part + (both[rows:, :width] + both[rows:, width:])


def dot_nt(a, b):
    return lax.dot_general(
        a, b, (((1,), (1,)), ((), ())), precision=HIGH, preferred_element_type=F32
    )


def dot_nn(a, b):
    return jnp.dot(a, b, precision=HIGH, preferred_element_type=F32)


def normalise(gram, rows):
    count = gram.shape[0]
    tall = lax.broadcasted_iota(jnp.int32, (count, 1), 0)
    row_id = lax.broadcasted_iota(jnp.int32, rows.shape, 0)
    for j in range(count):
        inverse = 1.0 / jnp.sqrt(gram[j : j + 1, j : j + 1])
        column = jnp.where(tall > j, gram[:, j : j + 1] * inverse, 0.0)
        across = gram[j : j + 1, :] * inverse
        pivot = rows[j : j + 1, :] * inverse
        rows = jnp.where(row_id == j, jnp.broadcast_to(pivot, rows.shape), rows - column * pivot)
        gram = gram - column * across
    return rows


def kernel(
    lay,
    total_len,
    cur_ref,
    prior_ref,
    diag_ref,
    tiles_hbm,
    where_ref,
    count_ref,
    out_ref,
    tiles,
    w_cols,
    w_rows,
    vec,
    far_in,
    col_in,
    terms,
    near_got,
    partial,
    far_got,
    col_terms,
    col_got,
    sums,
    fold_got,
    y_got,
    z_got,
    gb_sums,
    gb_fold,
    gb_y,
    gb_z,
    basis,
    cross,
    gmat,
    tile_sem,
    recv,
    gb_recv,
    sent,
    gb_sent,
):
    p = Place(lay)
    y_lo, z_far = lay["y_lo"], lay["z_far"]
    far = y_lo * z_far
    slots = tiles.shape[0]
    width = tiles.shape[1]
    k_rows = cur_ref.shape[0]

    barrier = pltpu.get_barrier_semaphore()
    greet = [p.at_z(dz) for dz in range(1, p.nz)]
    greet += [p.at_far(d, dy) for d in range(z_far) for dy in range(1, y_lo)]
    greet += [p.at_col(k) for k in range(1, p.ncol)]
    for k in range(1, p.ny):
        if k != y_lo and lay["y_hi"] > 1:
            greet.append(p.at_y(k))
    for device in greet:
        pl.semaphore_signal(barrier, inc=1, device_id=device, device_id_type=MESH)

    fetch = pltpu.make_async_copy(tiles_hbm, tiles, tile_sem)
    fetch.start()

    n_basis = prior_ref.shape[0] + k_rows
    basis[...] = jnp.zeros(basis.shape, F32)
    cross[...] = jnp.zeros(cross.shape, F32)
    gmat[...] = jnp.zeros(gmat.shape, F32)
    basis[0, k_rows : n_basis] = prior_ref[...]
    basis[0, n_basis : n_basis + k_rows] = cur_ref[...]
    own = dot_nt(basis[0, k_rows : n_basis + k_rows], basis[0])
    packed = own[0:16] + pltpu.roll(own[16:32], 40, 1)
    packed = packed + jnp.concatenate(
        [pltpu.roll(own[32:40], 80, 1), jnp.zeros((8, width), F32)], axis=0
    )
    gb_sums[0] = packed
    vec[0] = cur_ref[...]
    far_in[0, 0, 0] = cur_ref[...]
    col_in[0, 0] = cur_ref[...]

    pl.semaphore_wait(barrier, len(greet))

    def send(src, dst, send_sem, recv_sem, device):
        pltpu.make_async_remote_copy(
            src_ref=src,
            dst_ref=dst,
            send_sem=send_sem,
            recv_sem=recv_sem,
            device_id=device,
            device_id_type=MESH,
        ).start()

    def wait_for(ref, sem):
        pltpu.make_async_copy(ref, ref, sem).wait()

    far_order = [d for d in (2, 1, 3) if d < z_far] + [0]
    near_order = [d for d in (0, 1, 3, 2) if d < z_far]

    def gather_start(s):
        for d in far_order:
            for dy in range(y_lo):
                if d or dy:
                    send(
                        vec.at[s],
                        far_in.at[s, 0, d * y_lo + dy],
                        sent.at[s, 0],
                        recv.at[s, d],
                        p.at_far(d, dy),
                    )
        for k in range(1, p.ncol):
            send(vec.at[s], col_in.at[s, k], sent.at[s, 1], recv.at[s, 4], p.at_col(k))

    def gather_rest(s):
        for d in near_order:
            first = 1 if d == 0 else 0
            arrived = far_in.at[s, 0, pl.ds(d * y_lo + first, y_lo - first)]
            wait_for(arrived, recv.at[s, d])
            chunk = pl.ds(d * y_lo, y_lo)
            for q, dz in enumerate(p.near_out()):
                send(
                    far_in.at[s, 0, chunk],
                    far_in.at[s, 1 + q, chunk],
                    sent.at[s, 2],
                    recv.at[s, 5],
                    p.at_z(dz),
                )
        wait_for(col_in.at[s, pl.ds(1, p.ncol - 1)], recv.at[s, 4])
        wait_for(far_in.at[s, pl.ds(1, 3)], recv.at[s, 5])

    def all_sum_stage(s, stage, value, got, ids, sem_s, sem_r, source):
        source[stage] = value
        for k, device in enumerate(ids):
            send(source.at[stage], got.at[k], sem_s, sem_r, device)

    def all_sum_wait(value, got, count, sem_r):
        wait_for(got, sem_r)
        total = value
        for k in range(count):
            total = total + got[k]
        return total

    fold_ids = [p.at_fold(k) for k in range(1, p.fold)]
    y_ids = [p.at_y(k) for k in range(1, p.ny)]
    z_ids = [p.at_z(k) for k in range(1, p.nz)]

    gather_start(0)
    for k, device in enumerate(fold_ids):
        send(gb_sums.at[0], gb_fold.at[k], gb_sent.at[0], gb_recv.at[0], device)

    fetch.wait()
    count = count_ref[0, 0]

    def prepare(t, carry):
        tile = tiles[t]
        tile = jnp.where(t < count, tile, jnp.zeros_like(tile))
        high, low = split(tile)
        w_cols[t] = jnp.concatenate([high, low], axis=1)
        high, low = split(tile.T)
        w_rows[t] = jnp.concatenate([high, low], axis=1)
        return carry

    lax.fori_loop(0, slots, prepare, 0)

    near_out, near_in = p.near_out(), p.near_in()
    row_slot, far_slot, row_goal, far_goal = [], [], [], []
    for t in range(slots):
        at_row, at_col = where_ref[0, t], where_ref[1, t]
        row_slot.append(lax.rem(p.c - at_row + p.ncol, p.ncol))
        row_goal.append(lax.rem(at_row - p.c + p.ncol, p.ncol))
        y_t = lax.div(at_col, p.nz)
        z_t = lax.rem(at_col, p.nz)
        far_t = lax.div(z_t, NEAR)
        near_t = lax.rem(z_t, NEAR)
        slot = jnp.int32(0)
        goals = []
        dy_in = lax.rem(p.y - y_t + y_lo, y_lo)
        dy_out = lax.rem(y_t - p.y + y_lo, y_lo)
        for q in range(4):
            z_from = p.z if q == 0 else lax.rem(p.z + near_in[q - 1], p.nz)
            z_to = p.z if q == 0 else lax.rem(p.z + near_out[q - 1], p.nz)
            d_in = lax.rem(lax.div(z_from, NEAR) - far_t + z_far, z_far)
            here = q * far + d_in * y_lo + dy_in
            slot = jnp.where(lax.rem(z_from, NEAR) == near_t, here, slot)
            d_out = lax.rem(far_t - lax.div(z_to, NEAR) + z_far, z_far)
            there = d_out * y_lo + dy_out
            goals.append(jnp.where(lax.rem(z_to, NEAR) == near_t, there, -1))
        far_slot.append(slot)
        far_goal.append(goals)
    block_id = lax.broadcasted_iota(jnp.int32, (y_lo, k_rows, width), 0)
    col_id = lax.broadcasted_iota(jnp.int32, (p.ncol, k_rows, width), 0)

    def multiply(s):
        flat = far_in.at[s]
        to_cols = [apply_tile(col_in[s, row_slot[t]], w_cols[t]) for t in range(slots)]
        for d in far_order:
            for q in (1, 2, 3, 0):
                block = jnp.zeros(block_id.shape, F32)
                for t in range(slots):
                    hit = block_id == far_goal[t][q] - d * y_lo
                    block = block + jnp.where(hit, to_cols[t][None], 0.0)
                chunk = pl.ds(d * y_lo, y_lo)
                terms[s, q, chunk] = block
                if q:
                    send(
                        terms.at[s, q, chunk],
                        near_got.at[s, q - 1, chunk],
                        sent.at[s, 3],
                        recv.at[s, 6 + d],
                        p.at_z(near_out[q - 1]),
                    )
        block = jnp.zeros(col_id.shape, F32)
        for t in range(slots):
            q_t = lax.div(far_slot[t], far)
            to_rows = apply_tile(flat[q_t, lax.rem(far_slot[t], far)], w_rows[t])
            block = block + jnp.where(col_id == row_goal[t], to_rows[None], 0.0)
        col_terms[s] = block
        for k in range(1, p.ncol):
            send(col_terms.at[s, k], col_got.at[s, k - 1], sent.at[s, 4], recv.at[s, 10], p.at_col(k))

    def collect(s):
        for d in far_order:
            chunk = pl.ds(d * y_lo, y_lo)
            wait_for(near_got.at[s, pl.ds(0, 3), chunk], recv.at[s, 6 + d])
            total = terms[s, 0, chunk]
            for q in range(3):
                total = total + near_got[s, q, chunk]
            partial[s, chunk] = total
            for dy in range(y_lo):
                if d or dy:
                    at = d * y_lo + dy
                    send(partial.at[s, at], far_got.at[s, at - 1], sent.at[s, 5], recv.at[s, 11], p.at_far(d, dy))
        image = diag_ref[...] * vec[s] + col_terms[s, 0] + partial[s, 0]
        wait_for(col_got.at[s], recv.at[s, 10])
        for k in range(p.ncol - 1):
            image = image + col_got[s, k]
        wait_for(far_got.at[s], recv.at[s, 11])
        for k in range(far - 1):
            image = image + far_got[s, k]
        return image

    def gb_stage(value, stage, ids, got):
        gb_sums[stage] = value
        for k, device in enumerate(ids):
            send(gb_sums.at[stage], got.at[k], gb_sent.at[stage], gb_recv.at[stage], device)

    def gb_total(stage, got, n):
        wait_for(got, gb_recv.at[stage])
        total = gb_sums[stage]
        for k in range(n):
            total = total + got[k]
        return total

    lane = lax.broadcasted_iota(jnp.int32, (k_rows, width), 1)
    in_basis = (lane >= k_rows) & (lane < k_rows + n_basis)

    for s in range(2):
        if s:
            gather_start(s)
        gather_rest(s)
        multiply(s)
        if s == 0:
            gb_stage(gb_total(0, gb_fold, p.fold - 1), 1, y_ids, gb_y)
        image = collect(s)
        basis[s, 0:k_rows] = image
        value = dot_nt(image, basis[s])
        if s:
            value = value + dot_nt(vec[s], cross[...])
        all_sum_stage(s, 0, value, fold_got.at[s], fold_ids, sent.at[s, 6], recv.at[s, 12], sums.at[s])
        if s == 0:
            gb_stage(gb_total(1, gb_y, p.ny - 1), 2, z_ids, gb_z)
        value = all_sum_wait(value, fold_got.at[s], p.fold - 1, recv.at[s, 12])
        all_sum_stage(s, 1, value, y_got.at[s], y_ids, sent.at[s, 7], recv.at[s, 13], sums.at[s])
        value = all_sum_wait(value, y_got.at[s], p.ny - 1, recv.at[s, 13])
        all_sum_stage(s, 2, value, z_got.at[s], z_ids, sent.at[s, 8], recv.at[s, 14], sums.at[s])
        if s == 0:
            packed = gb_total(2, gb_z, p.nz - 1)
            wide = lax.broadcasted_iota(jnp.int32, packed.shape, 1)
            keep = (wide >= 8) & (wide < 48)
            gmat[0, 8:24] = jnp.where(keep, packed, 0.0)
            gmat[0, 24:40] = jnp.where(keep, pltpu.roll(packed, width - 40, 1), 0.0)
            gmat[0, 40:48] = jnp.where(keep, pltpu.roll(packed, width - 80, 1), 0.0)[0:8]
        value = all_sum_wait(value, z_got.at[s], p.nz - 1, recv.at[s, 14])

        inner = jnp.where(in_basis, value, 0.0)
        proj = inner * (1.0 / total_len)
        if s:
            newest = jnp.where(in_basis, pltpu.roll(value, width - 64, 1), 0.0)
            gmat[1, 40:48] = jnp.where(lane < 40, newest, 0.0)
            gmat[2, 40:48] = newest
            swept = dot_nn(proj, gmat[1]) + dot_nt(proj, gmat[2])
        else:
            swept = dot_nn(proj, gmat[0])
        gram = (value[:, 0:k_rows] + dot_nt(swept - 2.0 * inner, proj)) * (1.0 / total_len)
        remainder = image - dot_nn(proj, basis[s])
        fresh = normalise(gram, remainder)
        out_ref[s * k_rows : (s + 1) * k_rows] = fresh
        if s == 0:
            vec[1] = fresh
            far_in[1, 0, 0] = fresh
            col_in[1, 0] = fresh
            basis[1, 8:32] = prior_ref[8:32]
            basis[1, 32:40] = cur_ref[...]
            basis[1, 40:48] = fresh
            cross[72:112] = basis[1, 8:48]
            old = pltpu.roll(gmat[0, 16:48], width - 8, 1)
            wide = lax.broadcasted_iota(jnp.int32, old.shape, 1)
            gmat[1, 8:40] = jnp.where((wide >= 8) & (wide < 40), old, 0.0)

    for s in range(2):
        wait_for(far_in.at[s, 0, pl.ds(0, far - 1)], sent.at[s, 0])
        wait_for(col_in.at[s, pl.ds(1, p.ncol - 1)], sent.at[s, 1])
        wait_for(far_in.at[s, pl.ds(1, 3)], sent.at[s, 2])
        wait_for(near_got.at[s], sent.at[s, 3])
        wait_for(col_got.at[s], sent.at[s, 4])
        wait_for(far_got.at[s], sent.at[s, 5])
        wait_for(fold_got.at[s], sent.at[s, 6])
        wait_for(y_got.at[s], sent.at[s, 7])
        wait_for(z_got.at[s], sent.at[s, 8])
    wait_for(gb_fold, gb_sent.at[0])
    wait_for(gb_y, gb_sent.at[1])
    wait_for(gb_z, gb_sent.at[2])


def body(lay, total_len, current_block, prior_blocks, diagonal, stored_tiles, tile_coords, tile_counts):
    k_rows, width = current_block.shape
    slots = stored_tiles.shape[2]
    far = lay["y_lo"] * lay["z_far"]
    fold = lay["x"] * lay["core"]
    ncol = lay["y_hi"] * fold
    ny = lay["y_lo"] * lay["y_hi"]
    nz = lay["z_far"] * NEAR
    one = (k_rows, width)
    vmem = pl.BlockSpec(memory_space=pltpu.VMEM)
    smem = pl.BlockSpec(memory_space=pltpu.SMEM)
    scratch = [
        pltpu.VMEM((slots, width, width), F32),
        pltpu.VMEM((slots, width, 2 * width), BF16),
        pltpu.VMEM((slots, width, 2 * width), BF16),
        pltpu.VMEM((2, *one), F32),
        pltpu.VMEM((2, 4, far, *one), F32),
        pltpu.VMEM((2, ncol, *one), F32),
        pltpu.VMEM((2, 4, far, *one), F32),
        pltpu.VMEM((2, 3, far, *one), F32),
        pltpu.VMEM((2, far, *one), F32),
        pltpu.VMEM((2, far - 1, *one), F32),
        pltpu.VMEM((2, ncol, *one), F32),
        pltpu.VMEM((2, ncol - 1, *one), F32),
        pltpu.VMEM((2, 3, *one), F32),
        pltpu.VMEM((2, fold - 1, *one), F32),
        pltpu.VMEM((2, ny - 1, *one), F32),
        pltpu.VMEM((2, nz - 1, *one), F32),
        pltpu.VMEM((3, 2 * k_rows, width), F32),
        pltpu.VMEM((fold - 1, 2 * k_rows, width), F32),
        pltpu.VMEM((ny - 1, 2 * k_rows, width), F32),
        pltpu.VMEM((nz - 1, 2 * k_rows, width), F32),
        pltpu.VMEM((2, width, width), F32),
        pltpu.VMEM((width, width), F32),
        pltpu.VMEM((3, width, width), F32),
        pltpu.SemaphoreType.DMA,
        pltpu.SemaphoreType.DMA((2, 15)),
        pltpu.SemaphoreType.DMA((3,)),
        pltpu.SemaphoreType.DMA((2, 9)),
        pltpu.SemaphoreType.DMA((3,)),
    ]
    return pl.pallas_call(
        functools.partial(kernel, lay, total_len),
        out_shape=jax.ShapeDtypeStruct((2 * k_rows, width), F32),
        in_specs=[vmem, vmem, vmem, pl.BlockSpec(memory_space=pl.ANY), smem, smem],
        out_specs=vmem,
        scratch_shapes=scratch,
        compiler_params=pltpu.CompilerParams(
            collective_id=0, has_side_effects=True, vmem_limit_bytes=24 * 1024 * 1024
        ),
        name="lanczos",
    )(
        current_block,
        prior_blocks,
        diagonal[None, :],
        stored_tiles[0, 0],
        tile_coords[0, 0],
        tile_counts,
    )


def build(mesh, lay):
    total_len = float(128 * mesh.shape["row"] * mesh.shape["col"])
    in_specs = (
        P(None, ("row", "col")),
        P(None, ("row", "col")),
        P(("row", "col")),
        P("row", "col", None, None, None),
        P("row", "col", None, None),
        P("row", "col"),
    )
    return jax.shard_map(
        functools.partial(body, lay, total_len),
        mesh=mesh,
        in_specs=in_specs,
        out_specs=P(None, ("row", "col")),
        check_vma=False,
    )


def solution(mesh):
    return build(mesh, LAYOUT)
```

time: 1640 us -> 114 us (0.07)
  blocking collectives: 920 us -> 0 us
  waiting for transfers between devices: 689 us -> 0 us
  Pallas kernels: 0 us -> 110 us
    reduce_scatter x4 -> x0, waiting for transfers between devices: 689 us -> none  [the longest x2 531 us: column_total(): return lax.psum_scatter(col_terms, 'row', scatter_dimension=1, tiled=True)]
    psum x4 -> x0, blocking collectives: 575 us -> none  [grid_total(): return lax.psum(values, ('row', 'col'))]
    all_gather x4 -> x0, blocking collectives: 344 us -> none  [the longest x2 258 us: body(): column_vector = lax.all_gather(current, 'row', axis=1, tiled=True)]
    pallas_call x0 -> x1, Pallas kernels: none -> 110 us  [body(): pl.pallas_call(functools.partial(kernel, lay, total_len), out_shape=jax.S...]
  transfers between devices with their start and end apart: 4 -> 0, of which waited for: 4 -> 0; matrix products, arithmetic and copies ran while one was open for 0% -> 0% of each run, Pallas kernels for 0% -> 0%
where the time goes in v1:
time: 114 us
  Pallas kernels  110 us (96%)
  local copies, waits for them, and re-layouts  3.02 us (3%)
    pallas_call x1, Pallas kernels, body(): pl.pallas_call(functools.partial(kernel, lay, total_len), out_shape=jax.S...  110 us
    unnamed x11, local copies, waits for them, and re-layouts  3.02 us

profile of v1, /device:TPU:1, one launch (start us, length us, event | category | flops | bytes accessed | tf_op | source)
XLA Modules:
  0.0 113.8 jit_solution(4393909725850039527)
XLA Ops:
  0.0 0.0 copy-start.2
  0.7 0.0 copy-start.3
  0.7 0.0 copy-start.4
  0.7 0.0 copy-done.2
  0.7 0.7 copy-done.3
  1.3 0.0 copy-done.4
  1.4 0.0 copy-start
  1.4 1.0 copy-done
  2.4 0.0 copy-start.1
  2.4 0.7 copy-done.1
  3.1 110.1 %lanczos.1 = f32[16,128]{1,0:T(8,128)S(1)} custom-call(f32[8,128]{1,0:T(8,128)S(1)} %copy-done.2, f32[32,128]{1,0:T(8,128)S(1)} %copy-done.1, f32[1,128]{1,0:T(1,128)S(1)} %bitcast.5, f32[8,128,128]{2,1,0:T(8,128)S(1)} %bitcast.3, s32[2,8]{1,0:T(2,128)S(1)} %bitcast.4, s32[1,1]{1,0:T(1,128)S(6)} %copy.8.count_ref), custom_call_target="tpu_custom_call" | custom-call | tf_op jit(solution)/shard_map/lanczos/pallas_call | solution.py:468
  113.2 0.6 copy.9
Async XLA Ops:
  0.0 0.7 copy-start.2
  0.7 0.7 copy-start.3
  0.7 0.7 copy-start.4
  1.4 1.0 copy-start
  2.4 0.7 copy-start.1

commit v2 on v1

--- a/solution.py
+++ b/solution.py
@@ -120,8 +120,10 @@
     w_cols,
     w_rows,
     vec,
-    far_in,
-    col_in,
+    far_first,
+    far_second,
+    col_first,
+    col_second,
     terms,
     near_got,
     partial,
@@ -139,13 +141,21 @@
     basis,
     cross,
     gmat,
+    image_ref,
+    far_b,
+    col_b,
+    y_cols,
+    y_rows,
     tile_sem,
     recv,
     gb_recv,
     sent,
     gb_sent,
+    b_recv,
+    b_sent,
 ):
     p = Place(lay)
+    far_in, col_in = (far_first, far_second), (col_first, col_second)
     y_lo, z_far = lay["y_lo"], lay["z_far"]
     far = y_lo * z_far
     slots = tiles.shape[0]
@@ -178,8 +188,8 @@
     )
     gb_sums[0] = packed
     vec[0] = cur_ref[...]
-    far_in[0, 0, 0] = cur_ref[...]
-    col_in[0, 0] = cur_ref[...]
+    far_in[0][0, 0] = cur_ref[...]
+    col_in[0][0] = cur_ref[...]
 
     pl.semaphore_wait(barrier, len(greet))
 
@@ -200,35 +210,83 @@
     near_order = [d for d in (0, 1, 3, 2) if d < z_far]
 
     def gather_start(s):
+        source = image_ref if s else vec.at[0]
         for d in far_order:
             for dy in range(y_lo):
                 if d or dy:
                     send(
-                        vec.at[s],
-                        far_in.at[s, 0, d * y_lo + dy],
+                        source,
+                        far_in[s].at[0, d * y_lo + dy],
                         sent.at[s, 0],
                         recv.at[s, d],
                         p.at_far(d, dy),
                     )
         for k in range(1, p.ncol):
-            send(vec.at[s], col_in.at[s, k], sent.at[s, 1], recv.at[s, 4], p.at_col(k))
-
-    def gather_rest(s):
-        for d in near_order:
+            send(source, col_in[s].at[k], sent.at[s, 1], recv.at[s, 4], p.at_col(k))
+
+    def gather_chunks(s, order):
+        for d in order:
             first = 1 if d == 0 else 0
-            arrived = far_in.at[s, 0, pl.ds(d * y_lo + first, y_lo - first)]
+            arrived = far_in[s].at[0, pl.ds(d * y_lo + first, y_lo - first)]
             wait_for(arrived, recv.at[s, d])
             chunk = pl.ds(d * y_lo, y_lo)
             for q, dz in enumerate(p.near_out()):
                 send(
-                    far_in.at[s, 0, chunk],
-                    far_in.at[s, 1 + q, chunk],
+                    far_in[s].at[0, chunk],
+                    far_in[s].at[1 + q, chunk],
                     sent.at[s, 2],
                     recv.at[s, 5],
                     p.at_z(dz),
                 )
-        wait_for(col_in.at[s, pl.ds(1, p.ncol - 1)], recv.at[s, 4])
-        wait_for(far_in.at[s, pl.ds(1, 3)], recv.at[s, 5])
+
+    def gather_end(s):
+        wait_for(col_in[s].at[pl.ds(1, p.ncol - 1)], recv.at[s, 4])
+        wait_for(far_in[s].at[pl.ds(1, 3)], recv.at[s, 5])
+
+    direct = [d for d in range(z_far) if d != 2]
+    half = y_lo // 2
+
+    def prior_start():
+        if lay["y_hi"] > 1:
+            send(prior_ref, col_b.at[0, 1], b_sent.at[0], b_recv.at[0], p.at_col(p.fold))
+        for d in direct:
+            for dy in range(y_lo):
+                if d or dy:
+                    send(prior_ref, far_b.at[0, d * y_lo + dy], b_sent.at[1], b_recv.at[1 + d], p.at_far(d, dy))
+
+    def prior_near(d):
+        chunk = pl.ds(d * y_lo, y_lo)
+        for q, dz in enumerate(p.near_out()):
+            send(far_b.at[0, chunk], far_b.at[1 + q, chunk], b_sent.at[2], b_recv.at[5], p.at_z(dz))
+
+    def prior_middle():
+        if lay["y_hi"] > 1:
+            wait_for(col_b.at[0, 1], b_recv.at[0])
+        for k in range(1, p.fold):
+            send(col_b.at[0], col_b.at[k], b_sent.at[3], b_recv.at[6], p.at_fold(k))
+        for d in direct:
+            first = 1 if d == 0 else 0
+            wait_for(far_b.at[0, pl.ds(d * y_lo + first, y_lo - first)], b_recv.at[1 + d])
+        if z_far > 2:
+            for d, first in ((1, 0), (3, half)):
+                send(
+                    far_b.at[0, pl.ds(d * y_lo + first, half)],
+                    far_b.at[0, pl.ds(2 * y_lo + first, half)],
+                    b_sent.at[4],
+                    b_recv.at[3],
+                    p.at_far(d, 0),
+                )
+        for d in direct:
+            prior_near(d)
+
+    def prior_late():
+        if z_far > 2:
+            wait_for(far_b.at[0, pl.ds(2 * y_lo, y_lo)], b_recv.at[3])
+            prior_near(2)
+
+    def prior_end():
+        wait_for(col_b.at[pl.ds(1, p.fold - 1)], b_recv.at[6])
+        wait_for(far_b.at[pl.ds(1, 3)], b_recv.at[5])
 
     def all_sum_stage(s, stage, value, got, ids, sem_s, sem_r, source):
         source[stage] = value
@@ -247,6 +305,9 @@
     z_ids = [p.at_z(k) for k in range(1, p.nz)]
 
     gather_start(0)
+    far_b[0, 0] = prior_ref[...]
+    col_b[0, 0] = prior_ref[...]
+    prior_start()
     for k, device in enumerate(fold_ids):
         send(gb_sums.at[0], gb_fold.at[k], gb_sent.at[0], gb_recv.at[0], device)
 
@@ -265,10 +326,13 @@
     lax.fori_loop(0, slots, prepare, 0)
 
     near_out, near_in = p.near_out(), p.near_in()
-    row_slot, far_slot, row_goal, far_goal = [], [], [], []
+    row_slot, far_slot, row_goal, far_goal, row_part = [], [], [], [], []
     for t in range(slots):
         at_row, at_col = where_ref[0, t], where_ref[1, t]
         row_slot.append(lax.rem(p.c - at_row + p.ncol, p.ncol))
+        turn = lax.rem(p.c - at_row + p.ncol, p.fold)
+        away = jnp.where(lax.div(at_row, p.fold) == p.y_hi, 0, 1)
+        row_part.append((turn, away))
         row_goal.append(lax.rem(at_row - p.c + p.ncol, p.ncol))
         y_t = lax.div(at_col, p.nz)
         z_t = lax.rem(at_col, p.nz)
@@ -292,9 +356,23 @@
     block_id = lax.broadcasted_iota(jnp.int32, (y_lo, k_rows, width), 0)
     col_id = lax.broadcasted_iota(jnp.int32, (p.ncol, k_rows, width), 0)
 
-    def multiply(s):
-        flat = far_in.at[s]
-        to_cols = [apply_tile(col_in[s, row_slot[t]], w_cols[t]) for t in range(slots)]
+    def far_at(t):
+        return lax.div(far_slot[t], far), lax.rem(far_slot[t], far)
+
+    def widen(t):
+        turn, away = row_part[t]
+        q, at = far_at(t)
+        for got, old, weights, kept in (
+            (col_in[1][row_slot[t]], col_b[turn, away], w_cols, y_cols),
+            (far_in[1][q, at], far_b[q, at], w_rows, y_rows),
+        ):
+            kept[t, 0:40] = apply_tile(jnp.concatenate([got, old], axis=0), weights[t])
+
+    def multiply(s, mix):
+        if s:
+            to_cols = [dot_nn(mix, y_cols[t]) for t in range(slots)]
+        else:
+            to_cols = [apply_tile(col_in[0][row_slot[t]], w_cols[t]) for t in range(slots)]
         for d in far_order:
             for q in (1, 2, 3, 0):
                 block = jnp.zeros(block_id.shape, F32)
@@ -313,8 +391,13 @@
                     )
         block = jnp.zeros(col_id.shape, F32)
         for t in range(slots):
-            q_t = lax.div(far_slot[t], far)
-            to_rows = apply_tile(flat[q_t, lax.rem(far_slot[t], far)], w_rows[t])
+            if s:
+                to_rows = dot_nn(mix, y_rows[t])
+            else:
+                q, at = far_at(t)
+                to_rows = apply_tile(far_in[0][q, at], w_rows[t])
+                y_rows[t, 40:48] = to_rows
+                y_cols[t, 40:48] = to_cols[t]
             block = block + jnp.where(col_id == row_goal[t], to_rows[None], 0.0)
         col_terms[s] = block
         for k in range(1, p.ncol):
@@ -356,13 +439,14 @@
     lane = lax.broadcasted_iota(jnp.int32, (k_rows, width), 1)
     in_basis = (lane >= k_rows) & (lane < k_rows + n_basis)
 
+    gather_chunks(0, near_order)
+    gather_end(0)
+    mix = None
     for s in range(2):
-        if s:
-            gather_start(s)
-        gather_rest(s)
-        multiply(s)
+        multiply(s, mix)
         if s == 0:
             gb_stage(gb_total(0, gb_fold, p.fold - 1), 1, y_ids, gb_y)
+            prior_middle()
         image = collect(s)
         basis[s, 0:k_rows] = image
         value = dot_nt(image, basis[s])
@@ -370,18 +454,30 @@
             value = value + dot_nt(vec[s], cross[...])
         all_sum_stage(s, 0, value, fold_got.at[s], fold_ids, sent.at[s, 6], recv.at[s, 12], sums.at[s])
         if s == 0:
+            image_ref[...] = image
+            far_in[1][0, 0] = image
+            col_in[1][0] = image
+            gather_start(1)
             gb_stage(gb_total(1, gb_y, p.ny - 1), 2, z_ids, gb_z)
+            prior_late()
         value = all_sum_wait(value, fold_got.at[s], p.fold - 1, recv.at[s, 12])
         all_sum_stage(s, 1, value, y_got.at[s], y_ids, sent.at[s, 7], recv.at[s, 13], sums.at[s])
+        if s == 0:
+            gather_chunks(1, near_order[:1])
         value = all_sum_wait(value, y_got.at[s], p.ny - 1, recv.at[s, 13])
         all_sum_stage(s, 2, value, z_got.at[s], z_ids, sent.at[s, 8], recv.at[s, 14], sums.at[s])
         if s == 0:
+            gather_chunks(1, near_order[1:])
             packed = gb_total(2, gb_z, p.nz - 1)
             wide = lax.broadcasted_iota(jnp.int32, packed.shape, 1)
             keep = (wide >= 8) & (wide < 48)
             gmat[0, 8:24] = jnp.where(keep, packed, 0.0)
             gmat[0, 24:40] = jnp.where(keep, pltpu.roll(packed, width - 40, 1), 0.0)
             gmat[0, 40:48] = jnp.where(keep, pltpu.roll(packed, width - 80, 1), 0.0)[0:8]
+            prior_end()
+            gather_end(1)
+            for t in range(slots):
+                widen(t)
         value = all_sum_wait(value, z_got.at[s], p.nz - 1, recv.at[s, 14])
 
         inner = jnp.where(in_basis, value, 0.0)
@@ -394,13 +490,16 @@
         else:
             swept = dot_nn(proj, gmat[0])
         gram = (value[:, 0:k_rows] + dot_nt(swept - 2.0 * inner, proj)) * (1.0 / total_len)
-        remainder = image - dot_nn(proj, basis[s])
-        fresh = normalise(gram, remainder)
+        rows = image - dot_nn(proj, basis[s])
+        if s == 0:
+            unit = jnp.where(lane == lax.broadcasted_iota(jnp.int32, lane.shape, 0), 1.0, 0.0)
+            rows = jnp.concatenate([rows, unit - proj], axis=1)
+        rows = normalise(gram, rows)
+        fresh = rows[:, 0:width]
         out_ref[s * k_rows : (s + 1) * k_rows] = fresh
         if s == 0:
+            mix = rows[:, width : width + 48]
             vec[1] = fresh
-            far_in[1, 0, 0] = fresh
-            col_in[1, 0] = fresh
             basis[1, 8:32] = prior_ref[8:32]
             basis[1, 32:40] = cur_ref[...]
             basis[1, 40:48] = fresh
@@ -410,9 +509,9 @@
             gmat[1, 8:40] = jnp.where((wide >= 8) & (wide < 40), old, 0.0)
 
     for s in range(2):
-        wait_for(far_in.at[s, 0, pl.ds(0, far - 1)], sent.at[s, 0])
-        wait_for(col_in.at[s, pl.ds(1, p.ncol - 1)], sent.at[s, 1])
-        wait_for(far_in.at[s, pl.ds(1, 3)], sent.at[s, 2])
+        wait_for(far_in[s].at[0, pl.ds(0, far - 1)], sent.at[s, 0])
+        wait_for(col_in[s].at[pl.ds(1, p.ncol - 1)], sent.at[s, 1])
+        wait_for(far_in[s].at[pl.ds(1, 3)], sent.at[s, 2])
         wait_for(near_got.at[s], sent.at[s, 3])
         wait_for(col_got.at[s], sent.at[s, 4])
         wait_for(far_got.at[s], sent.at[s, 5])
@@ -422,6 +521,13 @@
     wait_for(gb_fold, gb_sent.at[0])
     wait_for(gb_y, gb_sent.at[1])
     wait_for(gb_z, gb_sent.at[2])
+    if lay["y_hi"] > 1:
+        wait_for(col_b.at[0, 1], b_sent.at[0])
+    wait_for(far_b.at[0, pl.ds(0, len(direct) * y_lo - 1)], b_sent.at[1])
+    wait_for(far_b.at[pl.ds(1, 3)], b_sent.at[2])
+    wait_for(col_b.at[pl.ds(1, p.fold - 1)], b_sent.at[3])
+    if z_far > 2:
+        wait_for(far_b.at[0, pl.ds(2 * y_lo, y_lo)], b_sent.at[4])
 
 
 def body(lay, total_len, current_block, prior_blocks, diagonal, stored_tiles, tile_coords, tile_counts):
@@ -440,8 +546,10 @@
         pltpu.VMEM((slots, width, 2 * width), BF16),
         pltpu.VMEM((slots, width, 2 * width), BF16),
         pltpu.VMEM((2, *one), F32),
-        pltpu.VMEM((2, 4, far, *one), F32),
-        pltpu.VMEM((2, ncol, *one), F32),
+        pltpu.VMEM((4, far, *one), F32),
+        pltpu.VMEM((4, far, *one), F32),
+        pltpu.VMEM((ncol, *one), F32),
+        pltpu.VMEM((ncol, *one), F32),
         pltpu.VMEM((2, 4, far, *one), F32),
         pltpu.VMEM((2, 3, far, *one), F32),
         pltpu.VMEM((2, far, *one), F32),
@@ -459,11 +567,18 @@
         pltpu.VMEM((2, width, width), F32),
         pltpu.VMEM((width, width), F32),
         pltpu.VMEM((3, width, width), F32),
+        pltpu.VMEM(one, F32),
+        pltpu.VMEM((4, far, 4 * k_rows, width), F32),
+        pltpu.VMEM((fold, lay["y_hi"], 4 * k_rows, width), F32),
+        pltpu.VMEM((slots, 48, width), F32),
+        pltpu.VMEM((slots, 48, width), F32),
         pltpu.SemaphoreType.DMA,
         pltpu.SemaphoreType.DMA((2, 15)),
         pltpu.SemaphoreType.DMA((3,)),
         pltpu.SemaphoreType.DMA((2, 9)),
         pltpu.SemaphoreType.DMA((3,)),
+        pltpu.SemaphoreType.DMA((7,)),
+        pltpu.SemaphoreType.DMA((5,)),
     ]
     return pl.pallas_call(
         functools.partial(kernel, lay, total_len),

time: 114 us -> 118 us (1.035)
  Pallas kernels: 110 us -> 114 us
    pallas_call x1, Pallas kernels: 110 us -> 114 us  [body(): pl.pallas_call(functools.partial(kernel, lay, total_len), out_shape=jax.S...]
where the time goes in v2:
time: 118 us
  Pallas kernels  114 us (97%)
  local copies, waits for them, and re-layouts  3.02 us (3%)
    pallas_call x1, Pallas kernels, body(): pl.pallas_call(functools.partial(kernel, lay, total_len), out_shape=jax.S...  114 us
    unnamed x11, local copies, waits for them, and re-layouts  3.02 us

profile of v2, /device:TPU:1, one launch (start us, length us, event | category | flops | bytes accessed | tf_op | source)
XLA Modules:
  0.0 117.8 jit_solution(8307957935256363475)
XLA Ops:
  0.0 0.0 copy-start.2
  0.7 0.0 copy-start.3
  0.7 0.0 copy-start.4
  0.7 0.0 copy-done.2
  0.7 0.7 copy-done.3
  1.3 0.0 copy-done.4
  1.4 0.0 copy-start
  1.4 1.0 copy-done
  2.4 0.0 copy-start.1
  2.4 0.7 copy-done.1
  3.1 114.1 %lanczos.1 = f32[16,128]{1,0:T(8,128)S(1)} custom-call(f32[8,128]{1,0:T(8,128)S(1)} %copy-done.2, f32[32,128]{1,0:T(8,128)S(1)} %copy-done.1, f32[1,128]{1,0:T(1,128)S(1)} %bitcast.5, f32[8,128,128]{2,1,0:T(8,128)S(1)} %bitcast.3, s32[2,8]{1,0:T(2,128)S(1)} %bitcast.4, s32[1,1]{1,0:T(1,128)S(6)} %copy.8.count_ref), custom_call_target="tpu_custom_call" | custom-call | tf_op jit(solution)/shard_map/lanczos/pallas_call | solution.py:583
  117.2 0.6 copy.9
Async XLA Ops:
  0.0 0.7 copy-start.2
  0.7 0.7 copy-start.3
  0.7 0.7 copy-start.4
  1.4 1.0 copy-start
  2.4 0.7 copy-start.1

commit v3 on v1

--- a/solution.py
+++ b/solution.py
@@ -97,7 +97,7 @@
     tall = lax.broadcasted_iota(jnp.int32, (count, 1), 0)
     row_id = lax.broadcasted_iota(jnp.int32, rows.shape, 0)
     for j in range(count):
-        inverse = 1.0 / jnp.sqrt(gram[j : j + 1, j : j + 1])
+        inverse = lax.rsqrt(gram[j : j + 1, j : j + 1])
         column = jnp.where(tall > j, gram[:, j : j + 1] * inverse, 0.0)
         across = gram[j : j + 1, :] * inverse
         pivot = rows[j : j + 1, :] * inverse
@@ -109,13 +109,16 @@
 def kernel(
     lay,
     total_len,
-    cur_ref,
-    prior_ref,
-    diag_ref,
+    cur_hbm,
+    prior_hbm,
+    diag_hbm,
     tiles_hbm,
     where_ref,
     count_ref,
     out_ref,
+    cur_ref,
+    prior_ref,
+    diag_ref,
     tiles,
     w_cols,
     w_rows,
@@ -152,6 +155,15 @@
     width = tiles.shape[1]
     k_rows = cur_ref.shape[0]
 
+    fetches = [
+        pltpu.make_async_copy(source, goal, tile_sem.at[i])
+        for i, (source, goal) in enumerate(
+            ((cur_hbm, cur_ref), (prior_hbm, prior_ref), (diag_hbm, diag_ref), (tiles_hbm, tiles))
+        )
+    ]
+    for fetch in fetches:
+        fetch.start()
+
     barrier = pltpu.get_barrier_semaphore()
     greet = [p.at_z(dz) for dz in range(1, p.nz)]
     greet += [p.at_far(d, dy) for d in range(z_far) for dy in range(1, y_lo)]
@@ -162,13 +174,12 @@
     for device in greet:
         pl.semaphore_signal(barrier, inc=1, device_id=device, device_id_type=MESH)
 
-    fetch = pltpu.make_async_copy(tiles_hbm, tiles, tile_sem)
-    fetch.start()
-
     n_basis = prior_ref.shape[0] + k_rows
     basis[...] = jnp.zeros(basis.shape, F32)
     cross[...] = jnp.zeros(cross.shape, F32)
     gmat[...] = jnp.zeros(gmat.shape, F32)
+    fetches[0].wait()
+    fetches[1].wait()
     basis[0, k_rows : n_basis] = prior_ref[...]
     basis[0, n_basis : n_basis + k_rows] = cur_ref[...]
     own = dot_nt(basis[0, k_rows : n_basis + k_rows], basis[0])
@@ -250,7 +261,8 @@
     for k, device in enumerate(fold_ids):
         send(gb_sums.at[0], gb_fold.at[k], gb_sent.at[0], gb_recv.at[0], device)
 
-    fetch.wait()
+    fetches[2].wait()
+    fetches[3].wait()
     count = count_ref[0, 0]
 
     def prepare(t, carry):
@@ -435,7 +447,11 @@
     one = (k_rows, width)
     vmem = pl.BlockSpec(memory_space=pltpu.VMEM)
     smem = pl.BlockSpec(memory_space=pltpu.SMEM)
+    anywhere = pl.BlockSpec(memory_space=pl.ANY)
     scratch = [
+        pltpu.VMEM(one, F32),
+        pltpu.VMEM((4 * k_rows, width), F32),
+        pltpu.VMEM((1, width), F32),
         pltpu.VMEM((slots, width, width), F32),
         pltpu.VMEM((slots, width, 2 * width), BF16),
         pltpu.VMEM((slots, width, 2 * width), BF16),
@@ -459,7 +475,7 @@
         pltpu.VMEM((2, width, width), F32),
         pltpu.VMEM((width, width), F32),
         pltpu.VMEM((3, width, width), F32),
-        pltpu.SemaphoreType.DMA,
+        pltpu.SemaphoreType.DMA((4,)),
         pltpu.SemaphoreType.DMA((2, 15)),
         pltpu.SemaphoreType.DMA((3,)),
         pltpu.SemaphoreType.DMA((2, 9)),
@@ -468,11 +484,11 @@
     return pl.pallas_call(
         functools.partial(kernel, lay, total_len),
         out_shape=jax.ShapeDtypeStruct((2 * k_rows, width), F32),
-        in_specs=[vmem, vmem, vmem, pl.BlockSpec(memory_space=pl.ANY), smem, smem],
+        in_specs=[anywhere, anywhere, anywhere, anywhere, smem, smem],
         out_specs=vmem,
         scratch_shapes=scratch,
         compiler_params=pltpu.CompilerParams(
-            collective_id=0, has_side_effects=True, vmem_limit_bytes=24 * 1024 * 1024
+            collective_id=0, has_side_effects=True, vmem_limit_bytes=60 * 1024 * 1024
         ),
         name="lanczos",
     )(

time: 114 us -> 113 us (level)
  local copies, waits for them, and re-layouts: 3.02 us -> 1.3 us
    unnamed x11 -> x1, local copies, waits for them, and re-layouts: 3.02 us -> 1.3 us
where the time goes in v3:
time: 113 us
  Pallas kernels  111 us (98%)
  local copies, waits for them, and re-layouts  1.3 us (1%)
    pallas_call x1, Pallas kernels, body(): pl.pallas_call(functools.partial(kernel, lay, total_len), out_shape=jax.S...  111 us

profile of v3, /device:TPU:1, one launch (start us, length us, event | category | flops | bytes accessed | tf_op | source)
XLA Modules:
  0.0 112.7 jit_solution(8458248584902992805)
XLA Ops:
  0.7 110.8 %lanczos.1 = f32[16,128]{1,0:T(8,128)} custom-call(f32[8,128]{1,0:T(8,128)} %cur_hbm.1, f32[32,128]{1,0:T(8,128)} %prior_hbm.1, f32[1,128]{1,0:T(1,128)} %bitcast.5, f32[8,128,128]{2,1,0:T(8,128)} %bitcast.3, s32[2,8]{1,0:T(2,128)} %bitcast.4, s32[1,1]{1,0:T(1,128)S(6)} %copy.8.count_ref), custom_call_target="tpu_custom_call" | custom-call | tf_op jit(solution)/shard_map/lanczos/pallas_call | solution.py:484
  111.4 1.3 %copy.9 = f32[16,128]{1,0:T(8,128)} copy(f32[16,128]{1,0:T(8,128)} %lanczos.1) | data formatting | bytes 16384
